TPU v7x, 512 devices: a whole 4x4x16 slice. The times are simulated.
512 devices in a mesh: hist: 256 (over z, x, y_lo, core), orb: 2 (over y_hi).
Axes of the slice: x: 4, y: 4 (y_hi: 2, y_lo: 2; y = y_hi * 2 + y_lo), z: 16, core: 2. Of those that a mesh axis runs over, the one named last changes fastest.
Arguments:
- g_hist: bfloat16 [512, 64, 32768], P('hist', 'orb'), may hold values from -6 to 6
- sigma_hist: bfloat16 [2, 64, 32768], P(None, None, 'hist'), may hold values from -0.03125 to 0.03125
- diag_inv: float32 [512, 64, 64], P('hist'), may hold values from -0.75 to 0.75
- previous: float32 [2, 512, 64, 64], P(None, 'hist', 'orb'), may hold values from -6 to 6
- block_of_slot: int32 [256], replicated, may hold values from 0 to 255, each once
- front_pos: int32 [2], replicated, may hold values from 256 to 511
Outputs:
- g_row: float32 [2, 512, 64, 64], P(None, 'hist', 'orb')
- sigma_row: float32 [2, 512, 64, 64], P(None, 'hist', 'orb')
Inputs may be any that keep to these rules, and one draw needn't show every extreme that they name: `block_of_slot`: every block index appears once.
All inputs are finite; a program needn't handle non-finite values.
Results may differ from a plain program's by a relative error of at most 0.0003.
Values may be sent and summed in bfloat16 or wider, within the bound.
No kernel may reach another device: no remote copies, remote signals or barrier semaphores. Data moves between devices by JAX's collectives and lax.ppermute only.
A program may use at most 64 MiB of HBM per device.

v0:
```python
import jax
import jax.numpy as jnp
from jax import lax
from jax.sharding import Mesh
from jax.sharding import PartitionSpec as P

HIST = ("hist_0", "hist_1", "hist_2", "hist_3")
COUPLING = 0.5


def from_root(value, axes, root):
    value = jnp.where(lax.axis_index(axes) == root, value, jnp.zeros_like(value))
    for axis in axes:
        value = lax.psum(value, axis)
    return value


def from_everyone(value, axis):
    count = lax.axis_size(axis)
    return lax.all_to_all(
        jnp.broadcast_to(value[None], (count, *value.shape)), axis, 0, 0, tiled=True
    )


def joined_along(blocks, dim):
    blocks = jnp.moveaxis(blocks, 0, dim)
    lengths = blocks.shape
    return blocks.reshape(*lengths[:dim], lengths[dim] * lengths[dim + 1], *lengths[dim + 2 :])


def gathered_copies(value, axis, dim):
    blocks = from_everyone(value, axis)
    return joined_along(blocks, dim)


def contract(g_piece, s_piece, times, col_time, front_pos):
    g_kept = jnp.where(
        (times[None, :] >= col_time[:, None])[:, None, :], g_piece, jnp.zeros_like(g_piece)
    )
    s_kept = jnp.where(
        (times[None, :] <= front_pos[:, None])[:, None, :], s_piece, jnp.zeros_like(s_piece)
    )
    return jnp.einsum("tcx,fax->ftca", g_kept, s_kept, preferred_element_type=jnp.float32)


def inverse_row(diag_inv, when, col_count):
    local = lax.dynamic_index_in_dim(diag_inv, when % col_count, 0, keepdims=False)
    return from_root(local, HIST, when // col_count)


def body(g_hist, sigma_hist, diag_inv, previous, block_of_slot, front_pos):
    col_count = g_hist.shape[0]
    half_cols = g_hist.shape[1]
    orb_width = sigma_hist.shape[1]
    orb_id = lax.axis_index("orb")
    slot_id = lax.axis_index(HIST)
    my_block = lax.dynamic_index_in_dim(block_of_slot, slot_id, 0, keepdims=False)
    col_time = my_block * col_count + jnp.arange(col_count, dtype=jnp.int32)
    piece = lax.all_gather(sigma_hist, HIST, axis=2, tiled=True)
    count = piece.shape[2]
    times = jnp.arange(count, dtype=jnp.int32) // orb_width
    integral = contract(g_hist, piece, times, col_time, front_pos)
    combined = previous + integral
    rows = jnp.stack([inverse_row(diag_inv, front_pos[front], col_count) for front in range(2)])
    g_row = jnp.einsum("ftcb,fab->ftca", combined, rows, precision=lax.Precision.HIGHEST)
    whole = gathered_copies(g_row, "orb", 2)
    mirror = jnp.swapaxes(lax.dynamic_slice_in_dim(whole, orb_id * half_cols, half_cols, 3), 2, 3)
    sigma_row = COUPLING * g_row * g_row * mirror
    return (g_row, sigma_row)


def solution(mesh):
    split = Mesh(
        mesh.devices.reshape(16, 4, 2, 2, mesh.shape["orb"]),
        ("hist_0", "hist_1", "hist_2", "hist_3", "orb"),
    )
    in_specs = (
        P(HIST, "orb", None),
        P(None, None, HIST),
        P(HIST, None, None),
        P(None, HIST, "orb", None),
        P(),
        P(),
    )
    out_specs = (P(None, HIST, "orb", None), P(None, HIST, "orb", None))
    return jax.shard_map(body, mesh=split, in_specs=in_specs, out_specs=out_specs, check_vma=False)
```

profile of v0, /device:TPU:2, one launch (start us, length us, event | category | flops | bytes accessed | tf_op | source)
XLA Modules:
  0.0 462.0 jit_solution(15964508195874430775)
XLA Ops:
  7.2 0.0 all-gather.2.cloned.1.call-start
  7.2 0.7 all-gather.2.cloned.1.call-update
  7.9 1.3 fusion.28
  14.5 1.3 dynamic_slice.14
  16.4 0.8 select_bitcast_fusion.1
  17.2 62.1 %all-reduce = (f32[64,64]{1,0:T(8,128)S(1)}, f32[64,64]{1,0:T(8,128)S(1)}) all-reduce(f32[64,64]{1,0:T(8,128)S(1)} %get-tuple-element.13, f32[64,64]{1,0:T(8,128)S(1)} %get-tuple-element.12), channel_id=1, replica_groups=mesh['hist_0'=16,'hist_1'=4,'hist_2'=2,'hist_3'=2,'orb'=2] {'hist_0'}, use_global_device_ids=true, to_apply=%region_4.5 | all-reduce | flops 8192 | bytes 65536 | tf_op jit(solution)/shard_map/psum | solution.py:14
  79.3 14.6 %all-reduce.1 = (f32[64,64]{1,0:T(8,128)S(1)}, f32[64,64]{1,0:T(8,128)S(1)}) all-reduce(f32[64,64]{1,0:T(8,128)S(1)} %get-tuple-element.2, f32[64,64]{1,0:T(8,128)S(1)} %get-tuple-element.3), channel_id=1, replica_groups=mesh['hist_0'=16,'hist_1'=4,'hist_2'=2,'hist_3'=2,'orb'=2] {'hist_1'}, use_global_device_ids=true, to_apply=%region_5.6 | all-reduce | flops 8192 | bytes 65536 | tf_op jit(solution)/shard_map/psum | solution.py:14
  94.0 8.9 %all-reduce.3 = (f32[64,64]{1,0:T(8,128)S(1)}, f32[64,64]{1,0:T(8,128)S(1)}) all-reduce(f32[64,64]{1,0:T(8,128)S(1)} %get-tuple-element.4, f32[64,64]{1,0:T(8,128)S(1)} %get-tuple-element.5), channel_id=1, replica_groups=mesh['hist_0'=16,'hist_1'=4,'hist_2'=2,'hist_3'=2,'orb'=2] {'hist_2'}, use_global_device_ids=true, to_apply=%region_6.7 | all-reduce | flops 8192 | bytes 65536 | tf_op jit(solution)/shard_map/psum | solution.py:14
  102.9 3.6 all-reduce.2
  106.6 1.0 broadcast_compare_fusion.1
  107.6 325.5 %all-gather.2.cloned.1.call-done = bf16[2,64,32768]{2,1,0:T(8,128)(2,1)} async-done(((bf16[2,64,128]{2,1,0:T(8,128)(2,1)}), bf16[2,64,32768]{2,1,0:T(8,128)(2,1)}) %all-gather.2.cloned.1.call-update) | async-done | bytes 8388624 | tf_op jit(solution)/shard_map/all_gather | solution.py:59
  433.0 8.8 %fusion.14 = f32[2,2,32,64]{3,2,1,0:T(8,128)S(1)} fusion(f32[2,2,32,64]{3,2,1,0:T(8,128)} %param.9, bf16[2,32,32768]{2,1,0:T(8,128)(2,1)} %param.6, pred[2,32768]{1,0:T(4,128)(4,1)S(1)} %get-tuple-element.11, bf16[2,64,32768]{2,1,0:T(8,128)(2,1)} %all-gather.2.cloned.1.call-done, pred[2,32768]{1,0:T(4,128)(4,1)S(1)} %get-tuple-element.10), kind=kOutput, calls=%fused_computation.10 | convolution fusion | flops 543170560 | bytes 12779520 | tf_op jit(solution)/shard_map/tcx,fax->ftca/dot_general | solution.py:43
  441.8 0.2 fusion.23
  442.0 0.0 copy-start
  442.1 0.8 reshape.83
  442.8 4.3 all-to-all-start
  447.2 5.6 %all-to-all-done = f32[2,1,8192]{2,1,0:T(1,128)S(1)} async-done(((f32[2,1,8192]{2,1,0:T(1,128)}), f32[2,1,8192]{2,1,0:T(1,128)S(1)}, u32[]{:S(2)}, u32[]{:S(2)}) %all-to-all-start) | async-done | bytes 65568 | tf_op jit(solution)/shard_map/all_to_all | solution.py:20
  452.8 0.5 broadcast.82
  453.3 0.8 reduce
  454.1 0.1 reshape.84
  454.3 0.1 constant_dynamic-slice_fusion
  454.4 0.1 copy.14
  454.5 0.6 fusion.22
  455.1 0.0 copy-done
  (4 shorter events, 0.0 us)
Async XLA Ops:
  7.2 425.9 %all-gather.2.cloned.1.call-start = ((), (), s32[]{:S(2)}) async-start(), calls=%async_computation.1 | async-start | bytes 8421376 | tf_op jit(solution)/shard_map/all_gather | solution.py:59
  442.0 13.1 %copy-start = (f32[2,2,32,64]{3,2,1,0:T(8,128)}, f32[2,2,32,64]{3,2,1,0:T(8,128)S(1)}, u32[]{:S(2)}) copy-start(f32[2,2,32,64]{3,2,1,0:T(8,128)S(1)} %fusion.23) | copy-start | bytes 98308
  442.8 9.9 %all-to-all-start = ((f32[2,1,8192]{2,1,0:T(1,128)}), f32[2,1,8192]{2,1,0:T(1,128)S(1)}, u32[]{:S(2)}, u32[]{:S(2)}) async-start(f32[2,1,8192]{2,1,0:T(1,128)} %reshape.83), calls=%async_computation | async-start | bytes 131072 | tf_op jit(solution)/shard_map/all_to_all | solution.py:20
Sparse Core Ops, SparseCore 0:
  10.1 422.8 all-gather.1
where the time goes:
time: 462 us
  waiting for transfers between devices  332 us (72%)
  blocking collectives  89.3 us (19%)
  between operations  20 us (4%)
  matrix products  9 us (2%)
    all_gather x1, waiting for transfers between devices, body(): piece = lax.all_gather(sigma_hist, HIST, axis=2, tiled=True)  325 us
    psum x4, blocking collectives, from_root(): value = lax.psum(value, axis)  89.3 us
  transfers between devices with their start and end apart: 2, of which 2 were waited for; matrix products, arithmetic and copies ran while one was open for 1% of the time, Pallas kernels for 0%

commit v1 on v0

--- a/solution.py
+++ b/solution.py
@@ -56,7 +56,10 @@
     slot_id = lax.axis_index(HIST)
     my_block = lax.dynamic_index_in_dim(block_of_slot, slot_id, 0, keepdims=False)
     col_time = my_block * col_count + jnp.arange(col_count, dtype=jnp.int32)
-    piece = lax.all_gather(sigma_hist, HIST, axis=2, tiled=True)
+    size = lax.axis_size(HIST)
+    pieces = jnp.stack([sigma_hist for _ in range(size)])
+    pieces = lax.all_to_all(pieces, HIST, split_axis=0, concat_axis=0)
+    piece = jnp.concatenate(pieces, axis=2)
     count = piece.shape[2]
     times = jnp.arange(count, dtype=jnp.int32) // orb_width
     integral = contract(g_hist, piece, times, col_time, front_pos)

time: 462 us -> 490 us (1.061)
  the two profiles are of different devices: /device:TPU:2 before, /device:TPU:1 now
where the time goes in v1:
time: 490 us; the launch traced here: 489 us
  blocking collectives  433 us (88%)
  starting transfers between devices  27.9 us (6%)
  local copies, waits for them, and re-layouts  8.91 us (2%)
  between operations  6.69 us (1%)
  matrix products  6.42 us (1%)
    psum x4, blocking collectives, from_root(): value = lax.psum(value, axis)  433 us
    all_to_all x1, starting transfers between devices, body(): pieces = lax.all_to_all(pieces, HIST, split_axis=0, concat_axis=0)  24.1 us
  transfers between devices with their start and end apart: 2, of which 1 were waited for; matrix products, arithmetic and copies ran while one was open for 0% of the time, Pallas kernels for 0%

profile of v1, /device:TPU:1, one launch (start us, length us, event | category | flops | bytes accessed | tf_op | source)
XLA Modules:
  0.0 489.5 jit_solution(6273568145058361111)
XLA Ops:
  0.6 6.1 %stack.8 = bf16[256,2,64,128]{3,2,1,0:T(8,128)(2,1)} broadcast(bf16[2,64,128]{2,1,0:T(8,128)(2,1)} %param.7), dimensions={1,2,3} | broadcast | bytes 8421376 | tf_op jit(solution)/shard_map/stack | solution.py:60
  6.7 0.0 copy-start.2
  6.7 0.0 copy-start.4
  6.7 0.0 copy-start.1
  6.7 0.0 copy-start.3
  6.8 24.1 %all-to-all-start = ((bf16[256,2,64,128]{3,2,1,0:T(8,128)(2,1)}), bf16[256,2,64,128]{3,2,1,0:T(8,128)(2,1)}, u32[]{:S(2)}, u32[]{:S(2)}) async-start(bf16[256,2,64,128]{3,2,1,0:T(8,128)(2,1)} %stack.8), calls=%async_computation | async-start | bytes 16777216 | tf_op jit(solution)/shard_map/all_to_all | solution.py:61
  30.8 0.0 copy-done.2
  30.8 0.6 fusion.29
  36.6 0.0 copy-done.4
  36.7 0.6 dynamic_slice.14
  37.9 0.0 copy-done.1
  37.9 390.4 %all-reduce = (f32[64,64]{1,0:T(8,128)S(1)}, f32[64,64]{1,0:T(8,128)S(1)}) all-reduce(f32[64,64]{1,0:T(8,128)S(1)} %get-tuple-element.13, f32[64,64]{1,0:T(8,128)S(1)} %get-tuple-element.12), channel_id=1, replica_groups=mesh['hist_0'=16,'hist_1'=4,'hist_2'=2,'hist_3'=2,'orb'=2] {'hist_0'}, use_global_device_ids=true, to_apply=%region_4.5 | all-reduce | flops 8192 | bytes 65536 | tf_op jit(solution)/shard_map/psum | solution.py:14
  428.3 13.3 %all-reduce.1 = (f32[64,64]{1,0:T(8,128)S(1)}, f32[64,64]{1,0:T(8,128)S(1)}) all-reduce(f32[64,64]{1,0:T(8,128)S(1)} %get-tuple-element.2, f32[64,64]{1,0:T(8,128)S(1)} %get-tuple-element.3), channel_id=1, replica_groups=mesh['hist_0'=16,'hist_1'=4,'hist_2'=2,'hist_3'=2,'orb'=2] {'hist_1'}, use_global_device_ids=true, to_apply=%region_5.6 | all-reduce | flops 8192 | bytes 65536 | tf_op jit(solution)/shard_map/psum | solution.py:14
  441.7 6.4 %all-reduce.3 = (f32[64,64]{1,0:T(8,128)S(1)}, f32[64,64]{1,0:T(8,128)S(1)}) all-reduce(f32[64,64]{1,0:T(8,128)S(1)} %get-tuple-element.4, f32[64,64]{1,0:T(8,128)S(1)} %get-tuple-element.5), channel_id=1, replica_groups=mesh['hist_0'=16,'hist_1'=4,'hist_2'=2,'hist_3'=2,'orb'=2] {'hist_2'}, use_global_device_ids=true, to_apply=%region_6.7 | all-reduce | flops 8192 | bytes 65536 | tf_op jit(solution)/shard_map/psum | solution.py:14
  448.0 23.1 %all-reduce.2 = (f32[1,64,64]{2,1,0:T(8,128)S(1)}, f32[1,64,64]{2,1,0:T(8,128)S(1)}) all-reduce(f32[1,64,64]{2,1,0:T(8,128)S(1)} %bitcast.55, f32[1,64,64]{2,1,0:T(8,128)S(1)} %bitcast.56), channel_id=1, replica_groups=mesh['hist_0'=16,'hist_1'=4,'hist_2'=2,'hist_3'=2,'orb'=2] {'hist_3'}, use_global_device_ids=true, to_apply=%region_7.8 | all-reduce | flops 8192 | bytes 65536 | tf_op jit(solution)/shard_map/psum | solution.py:14
  471.2 0.3 broadcast_compare_fusion.1
  471.5 0.0 all-to-all-done
  471.5 0.0 copy-done.3
  471.5 6.2 %fusion.15 = f32[2,2,32,64]{3,2,1,0:T(8,128)S(1)} fusion(f32[2,2,32,64]{3,2,1,0:T(8,128)S(1)} %copy-done.3, bf16[2,32,32768]{2,1,0:T(8,128)(2,1)} %param.6, pred[2,32768]{1,0:T(4,128)(4,1)S(1)} %get-tuple-element.11, pred[2,32768]{1,0:T(4,128)(4,1)S(1)} %get-tuple-element.10, bf16[256,2,64,128]{3,2,1,0:T(8,128)(2,1)} %all-to-all-done), kind=kOutput, calls=%fused_computation.11 | convolution fusion | flops 543170560 | bytes 12779520 | tf_op jit(solution)/shard_map/tcx,fax->ftca/dot_general | solution.py:43
  477.7 0.2 fusion.24
  478.0 0.0 copy-start
  478.0 0.8 reshape.93
  478.8 3.9 all-to-all-start.1
  482.6 4.5 all-to-all-done.1
  487.1 0.5 broadcast.84
  487.6 0.8 reduce
  488.5 0.1 reshape.94
  488.6 0.1 constant_dynamic-slice_fusion
  488.7 0.1 copy.17
  488.8 0.6 fusion.23
  489.5 0.0 copy-done
  (5 shorter events, 0.1 us)
Async XLA Ops:
  6.7 24.1 %copy-start.2 = (s32[2]{0:T(128)S(1)}, s32[2]{0:T(128)}, u32[]{:S(2)}) copy-start(s32[2]{0:T(128)} %param.11) | copy-start | bytes 28
  6.7 29.9 %copy-start.4 = (s32[256]{0:T(256)S(1)}, s32[256]{0:T(256)}, u32[]{:S(2)}) copy-start(s32[256]{0:T(256)} %param.10) | copy-start | bytes 3076
  6.7 31.2 %copy-start.1 = (f32[2,64,64]{2,1,0:T(8,128)S(1)}, f32[2,64,64]{2,1,0:T(8,128)}, u32[]{:S(2)}) copy-start(f32[2,64,64]{2,1,0:T(8,128)} %param.8) | copy-start | bytes 98308
  6.7 464.8 %copy-start.3 = (f32[2,2,32,64]{3,2,1,0:T(8,128)S(1)}, f32[2,2,32,64]{3,2,1,0:T(8,128)}, u32[]{:S(2)}) copy-start(f32[2,2,32,64]{3,2,1,0:T(8,128)} %param.9) | copy-start | bytes 98308
  6.8 464.8 %all-to-all-start = ((bf16[256,2,64,128]{3,2,1,0:T(8,128)(2,1)}), bf16[256,2,64,128]{3,2,1,0:T(8,128)(2,1)}, u32[]{:S(2)}, u32[]{:S(2)}) async-start(bf16[256,2,64,128]{3,2,1,0:T(8,128)(2,1)} %stack.8), calls=%async_computation | async-start | bytes 16777216 | tf_op jit(solution)/shard_map/all_to_all | solution.py:61
  478.0 11.5 %copy-start = (f32[2,2,32,64]{3,2,1,0:T(8,128)}, f32[2,2,32,64]{3,2,1,0:T(8,128)S(1)}, u32[]{:S(2)}) copy-start(f32[2,2,32,64]{3,2,1,0:T(8,128)S(1)} %fusion.24) | copy-start | bytes 98308
  478.8 8.4 %all-to-all-start.1 = ((f32[2,1,8192]{2,1,0:T(1,128)}), f32[2,1,8192]{2,1,0:T(1,128)S(1)}, u32[]{:S(2)}, u32[]{:S(2)}) async-start(f32[2,1,8192]{2,1,0:T(1,128)} %reshape.93), calls=%async_computation.1 | async-start | bytes 131072 | tf_op jit(solution)/shard_map/all_to_all | solution.py:20
